TPU v7x, 32 devices: a whole 2x2x4 slice. The times are simulated.
32 devices in a mesh: tm: 4 (over x, core), expert: 8 (over z, y).
Axes of the slice: x: 2, y: 2, z: 4, core: 2. Of those that a mesh axis runs over, the one named last changes fastest.
Arguments:
- tokens: bfloat16 [8, 32, 64, 1280], P('expert', 'tm'), may hold values from -6 to 6
- time_taps: float32 [3, 1280], replicated, may hold values from -3 to 3
- norm_gain: float32 [1280], replicated, may hold values from 0.5 to 1.5
- expert_ids: int32 [8, 2048, 2], P('expert'), may hold values from 0 to 7, as said below
- priority_ranks: int32 [8, 2048, 2], P('expert'), may hold values from 0 to 256, as said below
- keep_mask: int32 [8, 2048, 2], P('expert'), may hold values from 0 to 1, as said below
- gate_weights: float32 [8, 2048, 2], P('expert'), may hold values from 0.2 to 1
- up_weight: bfloat16 [8, 1280, 5120], P('expert', None, 'tm'), may hold values from -0.15625 to 0.15625
- down_weight: bfloat16 [8, 5120, 1280], P('expert', 'tm'), may hold values from -0.078125 to 0.078125
- attn_gain: float32 [1280], replicated, may hold values from 0.5 to 1.5
- qkv_weight: bfloat16 [3, 1280, 1280], P(None, None, 'tm'), may hold values from -0.15625 to 0.15625
Outputs:
- stream: bfloat16 [8, 32, 64, 1280], P('expert', 'tm')
- qkv_rows: bfloat16 [3, 8, 2048, 1280], P(None, 'expert', None, 'tm')
Inputs may be any that keep to these rules, and one draw needn't show every extreme that they name: `expert_ids`: the two experts of a token differ. priority_ranks[b, t, k] counts the assignments of clip b to the same expert that come earlier in batch-priority order, and is given as 256 where that count is 256 or more; every first choice of a clip comes before every second choice. Within a clip the kept assignments of one expert have distinct ranks. keep_mask is 1 exactly where priority_ranks < 256, so every expert receives at most 256 rows from each clip, and exactly 256 for some expert of every clip.
All inputs are finite; a program needn't handle non-finite values.
Results may differ from a plain program's by a relative error of at most 0.008.
Values may be sent and summed in bfloat16 or wider, within the bound.
No kernel may reach another device: no remote copies, remote signals or barrier semaphores. Data moves between devices by JAX's collectives and lax.ppermute only.
A program may use at most 128 MiB of HBM per device.

v0:
```python
import functools

import jax
import jax.numpy as jnp
from jax import lax
from jax.experimental import pallas as pl
from jax.experimental.pallas import tpu as pltpu
from jax.sharding import PartitionSpec as P

eps = 1e-06
bf16 = jnp.bfloat16
f32 = jnp.float32
HBM = pl.BlockSpec(memory_space=pl.ANY)
VMEM = pl.BlockSpec(memory_space=pltpu.VMEM)
SMEM = pl.BlockSpec(memory_space=pltpu.SMEM)


def call(kernel, out_shape, in_specs, out_specs, scratch, megabytes, flops, moved, *args):
    return pl.pallas_call(
        kernel,
        out_shape=out_shape,
        in_specs=in_specs,
        out_specs=out_specs,
        scratch_shapes=scratch,
        compiler_params=pltpu.CompilerParams(vmem_limit_bytes=megabytes << 20),
        cost_estimate=pl.CostEstimate(flops=3*flops, bytes_accessed=3*moved, transcendentals=0),
    )(*args)


def swap(value, axis, distance):
    count = lax.axis_size(axis)
    return lax.ppermute(value, axis, [(i, i ^ distance) for i in range(count)])


def after(value, *others):
    return lax.optimization_barrier((value, others))[0]


def tile_of(rows, most=512):
    return most if rows % most == 0 else rows


def places_kernel(half, experts, where_ref, ids_ref, ranks_ref, keep_ref, gate_ref, out_ref, back_ref):
    me, core = where_ref[0], where_ref[1]
    ids, ranks, kept = ids_ref[...] ^ me, ranks_ref[...], keep_ref[...] == 1
    own = ranks - core * half
    out_ref[...] = jnp.where(kept & (own >= 0) & (own < half), ids * half + own, -1)
    upper = jnp.where(ranks >= half, 1, 0)
    back = ((upper ^ core) * experts + ids) * half + ranks - upper * half
    table = [jnp.where(kept, back, -1).astype(f32), gate_ref[...]]
    filler = jnp.zeros((8 - 2 * ids.shape[0], ids.shape[1]), f32)
    back_ref[...] = jnp.concatenate(table + [filler], 0).T


def slot_places(where, ids, ranks, keep, gates, half, experts):
    choices, rows = ids.shape
    return call(
        functools.partial(places_kernel, half, experts),
        [
            jax.ShapeDtypeStruct((choices, rows), jnp.int32),
            jax.ShapeDtypeStruct((rows, 8), f32),
        ],
        [SMEM] + [VMEM] * 4,
        [VMEM] * 2,
        [],
        8,
        rows * 64,
        rows * 512,
        where,
        ids,
        ranks,
        keep,
        gates,
    )


def dispatch_kernel(blocks, patches, per, where_ref, taps_ref, place_ref, *refs):
    tokens, refs = refs[:blocks], refs[blocks:]
    base_ref, outs, (extended, mixed_ref, sems) = refs[0], refs[1:-3], refs[-3:]
    rows = tokens[0].shape[0]
    copies = [
        pltpu.make_async_copy(
            tokens[i],
            extended.at[pl.ds(pl.multiple_of(where_ref[i] * rows, rows), rows)],
            sems.at[i],
        )
        for i in range(blocks)
    ]
    for copy in copies:
        copy.start()
    for copy in copies:
        copy.wait()
    frames = blocks * rows // patches
    width = extended.shape[1]
    for left in range(0, width, 128):
        lanes = slice(left, min(left + 128, width))
        taps = [taps_ref[i : i + 1, lanes] for i in range(3)]

        def step(t, carry, lanes=lanes, taps=taps):
            earlier, before = carry
            start = pl.multiple_of(t * patches, patches)
            now = extended[pl.ds(start, patches), lanes].astype(f32)
            mixed = taps[0] * now + taps[1] * before + taps[2] * earlier
            mixed_ref[pl.ds(start, patches), lanes] = mixed.astype(bf16)
            return before, now

        first = extended[0:patches, lanes].astype(f32)
        second = extended[patches : 2 * patches, lanes].astype(f32)
        mixed_ref[0:patches, lanes] = (taps[0] * first).astype(bf16)
        mixed_ref[patches : 2 * patches, lanes] = (taps[0] * second + taps[1] * first).astype(bf16)
        lax.fori_loop(2, frames, step, (first, second), unroll=3)

    place = place_ref[...]
    together = max(1, 512 // per)
    for base in range(0, len(outs), together):
        group = outs[base : base + together]
        size = per * len(group)
        slots = lax.broadcasted_iota(jnp.int32, (size, blocks * rows), 0) + base * per
        hit = (slots == place[0:1]) | (slots == place[1:2])
        picked = jnp.dot(
            jnp.where(hit, 1.0, 0.0).astype(bf16), mixed_ref[...], preferred_element_type=f32
        ).astype(bf16)
        for i, out in enumerate(group):
            out[...] = picked[i * per : (i + 1) * per]
    for i in range(blocks // 2):
        start = pl.multiple_of(where_ref[blocks + i] * rows, rows)
        base_ref[i * rows : (i + 1) * rows] = mixed_ref[pl.ds(start, rows)]


def mix_and_dispatch(where, taps, place, tokens, patches, experts, per):
    blocks = len(tokens)
    rows, cols = tokens[0].shape
    total = blocks * rows
    return call(
        functools.partial(dispatch_kernel, blocks, patches, per),
        [jax.ShapeDtypeStruct((total // 2, cols), bf16)]
        + [jax.ShapeDtypeStruct((per, cols), bf16)] * experts,
        [SMEM, VMEM, VMEM] + [HBM] * blocks,
        [VMEM] * (1 + experts),
        [
            pltpu.VMEM((total, cols), bf16),
            pltpu.VMEM((total, cols), bf16),
            pltpu.SemaphoreType.DMA((blocks,)),
        ],
        24,
        2 * total * per * experts * cols,
        total * cols * 2 + experts * per * cols * 2,
        where,
        taps,
        place,
        *tokens,
    )


def normalise(parts, starts, gain_ref, out):
    cols = parts[0].shape[1]
    scale = 1.0 / gain_ref.shape[1]
    values = [part.astype(f32) for part in parts]
    mean = sum(jnp.sum(value, -1, keepdims=True) for value in values) * scale
    values = [value - mean for value in values]
    spread = sum(jnp.sum(value * value, -1, keepdims=True) for value in values) * scale
    factor = lax.rsqrt(spread + eps)
    for value, start in zip(values, starts):
        at = pl.ds(start, cols)
        out[:, at] = (value * factor * gain_ref[:, at]).astype(bf16)


def in_place(chip, shares, cols, run):
    if cols % 128 == 0:
        run([pl.multiple_of((chip ^ d) * cols, 128) for d in range(shares)])
        return
    for i in range(shares):

        @pl.when(chip == i)
        def _(i=i):
            run([(i ^ d) * cols for d in range(shares)])


def expert_kernel(shares, where_ref, gain_ref, *refs):
    parts, refs = refs[:shares], refs[shares:]
    weights, refs = refs[:4], refs[4:]
    outs, refs = refs[:shares], refs[shares:]
    normed, hidden, held, sems = refs[0], refs[1], refs[2:6], refs[6]
    rows, cols = parts[0].shape
    copies = [
        pltpu.make_async_copy(weight, place, sems.at[i])
        for i, (weight, place) in enumerate(zip(weights, held))
    ]
    ups, downs = held[:2], held[2:]
    wide = ups[0].shape[1]
    step = 256 if wide % 256 == 0 else wide
    for copy in copies:
        copy.start()

    def run(starts):
        normalise([part[...] for part in parts], starts, gain_ref, normed)
        for i, up in enumerate(ups):
            copies[i].wait()
            for left in range(0, wide, step):
                product = jnp.dot(
                    normed[...], up[:, left : left + step], preferred_element_type=f32
                )
                at = i * wide + left
                hidden[:, at : at + step] = jax.nn.gelu(product).astype(bf16)
        copies[2].wait()
        copies[3].wait()
        for out, start in zip(outs, starts):
            at = pl.ds(start, cols)
            total = jnp.dot(hidden[:, :wide], downs[0][:, at], preferred_element_type=f32)
            total += jnp.dot(hidden[:, wide:], downs[1][:, at], preferred_element_type=f32)
            out[...] = total.astype(bf16)

    in_place(where_ref[0], shares, cols, run)


def expert_project(where, gain, parts, weights):
    rows, cols = parts[0].shape
    shares = len(parts)
    width, wide = weights[0].shape
    return call(
        functools.partial(expert_kernel, shares),
        [jax.ShapeDtypeStruct((rows, cols), bf16)] * shares,
        [SMEM, VMEM] + [VMEM] * shares + [HBM] * 4,
        [VMEM] * shares,
        [
            pltpu.VMEM((rows, width), bf16),
            pltpu.VMEM((rows, 2 * wide), bf16),
            pltpu.VMEM((width, wide), bf16),
            pltpu.VMEM((width, wide), bf16),
            pltpu.VMEM((wide, width), bf16),
            pltpu.VMEM((wide, width), bf16),
            pltpu.SemaphoreType.DMA((4,)),
        ],
        24,
        8 * rows * width * wide,
        8 * width * wide + rows * width * 4,
        where,
        gain,
        *parts,
        *weights,
    )


def sum_kernel(pieces, *refs):
    values, outs = refs[:pieces], refs[pieces:]
    rows = outs[0].shape[0]
    for i, out in enumerate(outs):
        at = slice(i * rows, (i + 1) * rows)
        total = values[0][at].astype(f32)
        for value in values[1:]:
            total = total + value[at].astype(f32)
        out[...] = total.astype(bf16)


def sum_blocks(values, blocks):
    rows, cols = values[0].shape
    return call(
        functools.partial(sum_kernel, len(values)),
        [jax.ShapeDtypeStruct((rows // blocks, cols), bf16)] * blocks,
        [VMEM] * len(values),
        [VMEM] * blocks,
        [],
        8,
        rows * cols * 2,
        rows * cols * 2 * (len(values) + 1),
        *values,
    )


def combine_kernel(firsts, blocks, where_ref, place_ref, base_ref, *refs):
    sources, outs = refs[: len(firsts)], refs[len(firsts) :]
    choices = 2
    rows = base_ref.shape[0] // blocks

    def add(i):
        at = pl.ds(i * rows if isinstance(i, int) else pl.multiple_of(i * rows, rows), rows)
        start = pl.multiple_of(where_ref[i] * rows, rows)
        table = place_ref[pl.ds(start, rows)]
        place, gate = table[:, :choices].astype(jnp.int32), table[:, choices : 2 * choices]
        total = base_ref[at].astype(f32)
        for first, source in zip(firsts, sources):
            many = source.shape[0]
            lanes = lax.broadcasted_iota(jnp.int32, (rows, many), 1) + first
            weight = jnp.zeros((rows, many), f32)
            for k in range(choices):
                weight = jnp.where(lanes == place[:, k : k + 1], gate[:, k : k + 1], weight)
            total = total + jnp.dot(weight.astype(bf16), source[...], preferred_element_type=f32)
        if len(outs) == 1:
            outs[0][at] = total
        else:
            outs[i][...] = total.astype(bf16)

    if len(outs) == 1:
        lax.fori_loop(0, blocks, lambda i, carry: (add(i), carry)[1], 0)
    else:
        for i in range(blocks):
            add(i)


def combine(where, places, base, sources, firsts, last):
    blocks = where.shape[0]
    rows, cols = base.shape
    many = sum(source.shape[0] for source in sources)
    shapes = [jax.ShapeDtypeStruct((rows, cols), f32)]
    if last:
        shapes = [jax.ShapeDtypeStruct((rows // blocks, cols), bf16)] * blocks
    return call(
        functools.partial(combine_kernel, firsts, blocks),
        shapes,
        [SMEM, VMEM, VMEM] + [VMEM] * len(sources),
        [VMEM] * len(shapes),
        [],
        20,
        2 * rows * many * cols,
        rows * cols * 6 + many * cols * 2,
        where,
        places,
        base,
        *sources,
    )


def qkv_kernel(shares, block, earlier, where_ref, gain_ref, weight_ref, *refs):
    parts, refs = refs[:shares], refs[shares + earlier :]
    out, refs = refs[0], refs[1:]
    if block is not None:
        stream, stage, stage_sem, refs = refs[0], refs[-2], refs[-1], refs[1:-2]
    normed, held, weights, sem, weight_sem = refs
    rows, cols = parts[0].shape
    heads = out.shape[1]
    loads = []
    for j in range(3):
        at = slice(j * heads, (j + 1) * heads)
        loads.append(
            pltpu.make_async_copy(weight_ref.at[at], weights.at[at], weight_sem.at[j])
        )
        loads[-1].start()

    to = pl.ds(pl.multiple_of(where_ref[1] * rows, rows), rows)
    copies = [
        pltpu.make_async_copy(
            held.at[j * heads : (j + 1) * heads], out.at[j, :, to], sem.at[j]
        )
        for j in range(3)
    ]
    tile = tile_of(rows, 256)

    def run(starts):
        if block is not None:
            @pl.when(where_ref[0] == block)
            def _():
                for part, start in zip(parts, starts):
                    stage[:, pl.ds(start, cols)] = part[...]
                pltpu.make_async_copy(stage, stream, stage_sem).start()

        for left in range(0, rows, tile):
            at = slice(left, left + tile)
            normalise([part[at] for part in parts], starts, gain_ref, normed.at[at])
        for load in loads:
            load.wait()
        for left in range(0, rows, tile):
            at = slice(left, left + tile)
            result = lax.dot_general(
                weights[...], normed[at], (((1,), (1,)), ((), ())), preferred_element_type=f32
            )
            held[:, at] = result.astype(bf16)
        for copy in copies:
            copy.start()

    in_place(where_ref[0], shares, cols, run)
    for copy in copies:
        copy.wait()
    if block is not None:

        @pl.when(where_ref[0] == block)
        def _():
            pltpu.make_async_copy(stage, stream, stage_sem).wait()


def qkv_project(where, gain, weight, parts, total, block, earlier):
    shares = len(parts)
    rows = parts[0].shape[0]
    wide, width = weight.shape
    shapes = [jax.ShapeDtypeStruct((3, wide // 3, total), bf16)]
    scratch = [
        pltpu.VMEM((rows, width), bf16),
        pltpu.VMEM((wide, rows), bf16),
        pltpu.VMEM((wide, width), bf16),
        pltpu.SemaphoreType.DMA((3,)),
        pltpu.SemaphoreType.DMA((3,)),
    ]
    if block is not None:
        shapes += [jax.ShapeDtypeStruct((rows, width), bf16)]
        scratch += [pltpu.VMEM((rows, width), bf16), pltpu.SemaphoreType.DMA]
    return pl.pallas_call(
        functools.partial(qkv_kernel, shares, block, len(earlier)),
        out_shape=shapes,
        in_specs=[SMEM, VMEM, pl.BlockSpec(memory_space=pltpu.HBM)]
        + [VMEM] * shares
        + [HBM] * len(earlier),
        out_specs=[HBM] * len(shapes),
        scratch_shapes=scratch,
        input_output_aliases={3 + shares + i: i for i in range(len(earlier))},
        compiler_params=pltpu.CompilerParams(vmem_limit_bytes=20 << 20),
        cost_estimate=pl.CostEstimate(
            flops=2 * rows * width * wide,
            bytes_accessed=rows * (width + wide) * 2 + width * wide * 2,
            transcendentals=0,
        ),
    )(where, gain, weight, *parts, *earlier)


def local(
    tokens,
    time_taps,
    norm_gain,
    expert_ids,
    priority_ranks,
    keep_mask,
    gate_weights,
    up_weight,
    down_weight,
    attn_gain,
    qkv_weight,
):
    frames_here, patches, width = tokens.shape[1:]
    members = lax.axis_size("tm")
    experts = lax.axis_size("expert")
    chips = members // 2
    cols = width // chips
    place = lax.axis_index("tm")
    chip, core = place // 2, place % 2
    me = lax.axis_index("expert")
    own_rows = frames_here * patches
    rows = own_rows * members
    capacity = rows * expert_ids.shape[2] // (2 * experts)
    half = capacity // 2

    def columns_of(value, d):
        return lax.dynamic_slice_in_dim(value, (chip ^ d) * cols, cols, value.ndim - 1)

    def rows_of(value, i):
        return lax.dynamic_slice_in_dim(value, (2 * i + core) * own_rows, own_rows, 1)

    own_tokens = tokens.reshape(own_rows, width)
    theirs = [columns_of(own_tokens, d) for d in range(1, chips)]
    mine = columns_of(after(own_tokens, *theirs), 0)
    near = [mine] + [swap(value, "tm", 2 * d) for d, value in enumerate(theirs, 1)]
    over = [swap(value, "tm", 1) for value in near]
    token_places = jnp.stack(
        [(chip ^ d) * 2 + core for d in range(chips)]
        + [(chip ^ d) * 2 + 1 - core for d in range(chips)]
    ).astype(jnp.int32)

    ups = [up_weight[0], swap(up_weight[0], "tm", 1)]
    downs = [down_weight[0], swap(down_weight[0], "tm", 1)]
    qkv_columns = pltpu.with_memory_space_constraint(
        jnp.swapaxes(qkv_weight, 1, 2).reshape(-1, width), pltpu.HBM
    )
    taps = columns_of(time_taps, 0)

    where_chip = chip.astype(jnp.int32)[None]
    blocks_here = jnp.stack([2 * i + core for i in range(chips)]).astype(jnp.int32)
    out_place, back_place = slot_places(
        jnp.stack([me, core]).astype(jnp.int32),
        expert_ids[0].T,
        priority_ranks[0].T,
        keep_mask[0].T,
        gate_weights[0].T,
        half,
        experts,
    )

    weights = ups + downs
    near, over, weights, out_place = lax.optimization_barrier((near, over, weights, out_place))
    base, *sent = mix_and_dispatch(
        jnp.concatenate([token_places, blocks_here]),
        taps,
        out_place,
        near + over,
        patches,
        experts,
        half,
    )

    middle = experts // 2
    bounds = [0, middle // 2, middle, middle + middle // 2, experts]
    groups = [range(*pair) for pair in zip(bounds, bounds[1:])]
    arrived = [sent[0]] + [swap(sent[k], "expert", k) for k in range(1, groups[2].stop)]
    partial_sums = []
    for group in groups:
        rows_in = jnp.concatenate([arrived[k] for k in group], 0)
        shares = [rows_in] + [swap(rows_in, "tm", 2 * d) for d in range(1, chips)]
        if not partial_sums:
            last = after([sent[k] for k in groups[3]], *shares[1:])
            arrived += [swap(value, "expert", k) for k, value in zip(groups[3], last)]
        else:
            shares = after(shares, *partial_sums[-1])
        partial_sums.append(expert_project(where_chip, norm_gain[None], shares, weights))

    returned = [None] * len(groups)
    received = [None] * len(groups)
    sent_back = [None] * len(groups)
    for g, follows in ((2, None), (3, None), (1, 2), (0, 3)):
        sums = list(partial_sums[g])
        if follows:
            sums = after(sums, *sent_back[follows])
        received[g] = [swap(sums[d], "tm", 2 * d) for d in range(1, chips)]
        sent_back[g] = sum_blocks([sums[0]] + received[g], len(groups[g]))
        returned[g] = [
            swap(block, "expert", k) if k else block for k, block in zip(groups[g], sent_back[g])
        ]
    for g in (1, 2, 3):
        returned[g] = after(returned[g], *received[0])
    back = [jnp.concatenate(blocks, 0) for blocks in returned]
    over_back = [swap(value, "tm", 1) for value in back]
    total = base
    steps = [[(2, 0), (2, 1)], [(0, 0), (1, 0), (3, 0)], [(0, 1), (1, 1), (3, 1)]]
    for step in steps:
        sources = [(over_back if side else back)[g] for g, side in step]
        firsts = [(side * experts + groups[g].start) * half for g, side in step]
        done = combine(blocks_here, back_place, total, sources, firsts, step is steps[-1])
        total = done[0]
    stream = list(done)
    qkv_rows, own_stream, before = [], [], None
    for i in range(chips):
        if before:
            stream[i] = after(stream[i], *before)
        pieces = [stream[i]] + [swap(stream[i], "tm", 2 * d) for d in range(1, chips)]
        before = pieces
        if i:
            pieces = after(pieces, *qkv_rows)
        other = [swap(piece, "tm", 1) for piece in pieces]
        where = jnp.stack([chip, 2 * i + core]).astype(jnp.int32)
        *qkv_rows, own = qkv_project(
            where, attn_gain[None], qkv_columns, pieces, rows, i, qkv_rows + own_stream
        )
        own_stream = [own]
        where = jnp.stack([chip, 2 * i + 1 - core]).astype(jnp.int32)
        qkv_rows = list(
            qkv_project(where, attn_gain[None], qkv_columns, other, rows, None, qkv_rows)
        )
    return (own_stream[0].reshape(tokens.shape), jnp.swapaxes(qkv_rows[0], 1, 2)[:, None])


def solution(mesh):
    in_specs = (
        P("expert", "tm", None, None),
        P(),
        P(),
        P("expert", None, None),
        P("expert", None, None),
        P("expert", None, None),
        P("expert", None, None),
        P("expert", None, "tm"),
        P("expert", "tm", None),
        P(),
        P(None, None, "tm"),
    )
    out_specs = (P("expert", "tm", None, None), P(None, "expert", None, "tm"))
    return jax.shard_map(local, mesh=mesh, in_specs=in_specs, out_specs=out_specs, check_vma=False)
```

profile of v0, /device:TPU:0, one launch (start us, length us, event | category | flops | bytes accessed | tf_op | source)
XLA Modules:
  0.0 175.5 jit_solution(3934006215305780502)
XLA Ops:
  2.0 3.0 %collective-permute-start = (bf16[512,640]{1,0:T(8,128)(2,1)S(1)}, bf16[512,640]{1,0:T(8,128)(2,1)}, u32[]{:S(2)}, u32[]{:S(2)}) collective-permute-start(bf16[512,640]{1,0:T(8,128)(2,1)S(1)} %constant_dynamic-slice_fusion.1), channel_id=1, source_target_pairs={{0,16},{8,24},{16,0},{24,8},{1,17},{9,25},{17,1},{25,9},{2,18},{10... | collective-permute-start | bytes 1966088 | tf_op jit(solution)/shard_map/ppermute | solution.py:32
  5.2 14.7 %collective-permute-done.refs_1_ = bf16[512,640]{1,0:T(8,128)(2,1)} collective-permute-done((bf16[512,640]{1,0:T(8,128)(2,1)S(1)}, bf16[512,640]{1,0:T(8,128)(2,1)}, u32[]{:S(2)}, u32[]{:S(2)}) %collective-permute-start) | collective-permute-done | bytes 655392 | tf_op jit(solution)/shard_map/ppermute | solution.py:32
  22.3 7.6 %shard_map.123 = (bf16[1024,640]{1,0:T(8,128)(2,1)S(1)}, bf16[128,640]{1,0:T(8,128)(2,1)S(1)}, bf16[128,640]{1,0:T(8,128)(2,1)S(1)}, bf16[128,640]{1,0:T(8,128)(...) custom-call(s32[6]{0:T(128)S(1)} %concatenate.28.where_ref, ...), custom_call_target="tpu_custom_call" | custom-call | flops 8053063680 | bytes 11796480 | tf_op jit(solution)/shard_map/pallas_call | solution.py:19
  33.6 2.9 %collective-permute-start.5 = (bf16[128,640]{1,0:T(8,128)(2,1)S(1)}, bf16[128,640]{1,0:T(8,128)(2,1)S(1)}, u32[]{:S(2)}, u32[]{:S(2)}) collective-permute-start(bf16[128,640]{1,0:T(8,128)(2,1)S(1)} %get-tuple-element.75), channel_id=1, source_target_pairs={{0,4},{1,5},{2,6},{3,7},{4,0},{5,1},{6,2},{7,3},{8,12},{9,13},{10,... | collective-permute-start | bytes 491528 | tf_op jit(solution)/shard_map/ppermute | solution.py:32
  39.3 6.3 %collective-permute-done.8 = bf16[128,640]{1,0:T(8,128)(2,1)S(1)} collective-permute-done((bf16[128,640]{1,0:T(8,128)(2,1)S(1)}, bf16[128,640]{1,0:T(8,128)(2,1)S(1)}, u32[]{:S(2)}, u32[]{:S(2)}) %collective-permute-start.8) | collective-permute-done | bytes 163872 | tf_op jit(solution)/shard_map/ppermute | solution.py:32
  48.6 3.1 %collective-permute-done.6 = bf16[128,640]{1,0:T(8,128)(2,1)S(1)} collective-permute-done((bf16[128,640]{1,0:T(8,128)(2,1)S(1)}, bf16[128,640]{1,0:T(8,128)(2,1)S(1)}, u32[]{:S(2)}, u32[]{:S(2)}) %collective-permute-start.6) | collective-permute-done | bytes 163872 | tf_op jit(solution)/shard_map/ppermute | solution.py:32
  53.3 4.3 %collective-permute-start.16 = (bf16[128,640]{1,0:T(8,128)(2,1)S(1)}, bf16[128,640]{1,0:T(8,128)(2,1)S(1)}, u32[]{:S(2)}, u32[]{:S(2)}) collective-permute-start(bf16[128,640]{1,0:T(8,128)(2,1)S(1)} %get-tuple-element.99), channel_id=1, source_target_pairs={{0,6},{1,7},{2,4},{3,5},{4,2},{5,3},{6,0},{7,1},{8,14},{9,15},{10,... | collective-permute-start | bytes 491528 | tf_op jit(solution)/shard_map/ppermute | solution.py:32
  57.6 6.0 %shard_map.124 = (bf16[256,640]{1,0:T(8,128)(2,1)S(1)}, bf16[256,640]{1,0:T(8,128)(2,1)S(1)}) custom-call(s32[1]{0:T(128)} %bitcast.where_ref, f32[1,1280]{1,0:T(1,128)S(1)} %broadcast_in_dim.7.gain_ref, bf16[256,640]{1,0:T(8,128)(2,1)S(1)} %constant_dynamic-update-slice_fusion.4.refs_0_, bf16[256,640]{1,0:T(8,128)(2,1)S(1)} %collective-permute-done.12.refs_1_, ...), custom_call_target="tpu_custom_call" | custom-call | flops 10066329600 | bytes 43253760 | tf_op jit(solution)/shard_map/pallas_call | solution.py:19
  63.6 6.2 %shard_map.125 = (bf16[256,640]{1,0:T(8,128)(2,1)S(1)}, bf16[256,640]{1,0:T(8,128)(2,1)S(1)}) custom-call(s32[1]{0:T(128)} %bitcast.where_ref, f32[1,1280]{1,0:T(1,128)S(1)} %broadcast_in_dim.7.gain_ref, bf16[256,640]{1,0:T(8,128)(2,1)S(1)} %constant_dynamic-update-slice_fusion.2.refs_0_, bf16[256,640]{1,0:T(8,128)(2,1)S(1)} %collective-permute-done.10.refs_1_, ...), custom_call_target="tpu_custom_call" | custom-call | flops 10066329600 | bytes 43253760 | tf_op jit(solution)/shard_map/pallas_call | solution.py:19
  70.0 6.0 %shard_map.126 = (bf16[256,640]{1,0:T(8,128)(2,1)S(1)}, bf16[256,640]{1,0:T(8,128)(2,1)S(1)}) custom-call(s32[1]{0:T(128)} %bitcast.where_ref, f32[1,1280]{1,0:T(1,128)S(1)} %broadcast_in_dim.7.gain_ref, bf16[256,640]{1,0:T(8,128)(2,1)S(1)} %constant_dynamic-update-slice_fusion.refs_0_, bf16[256,640]{1,0:T(8,128)(2,1)S(1)} %collective-permute-done.7.refs_1_, ...), custom_call_target="tpu_custom_call" | custom-call | flops 10066329600 | bytes 43253760 | tf_op jit(solution)/shard_map/pallas_call | solution.py:19
  78.0 6.2 %shard_map.128 = (bf16[256,640]{1,0:T(8,128)(2,1)S(1)}, bf16[256,640]{1,0:T(8,128)(2,1)S(1)}) custom-call(s32[1]{0:T(128)} %bitcast.where_ref, f32[1,1280]{1,0:T(1,128)S(1)} %broadcast_in_dim.7.gain_ref, bf16[256,640]{1,0:T(8,128)(2,1)S(1)} %constant_dynamic-update-slice_fusion.6.refs_0_, bf16[256,640]{1,0:T(8,128)(2,1)S(1)} %collective-permute-done.18.refs_1_, ...), custom_call_target="tpu_custom_call" | custom-call | flops 10066329600 | bytes 43253760 | tf_op jit(solution)/shard_map/pallas_call | solution.py:19
  86.4 8.5 %collective-permute-done.19.refs_1_ = bf16[256,640]{1,0:T(8,128)(2,1)S(1)} collective-permute-done((bf16[256,640]{1,0:T(8,128)(2,1)S(1)}, bf16[256,640]{1,0:T(8,128)(2,1)S(1)}, u32[]{:S(2)}, u32[]{:S(2)}) %collective-permute-start.19) | collective-permute-done | bytes 327712 | tf_op jit(solution)/shard_map/ppermute | solution.py:32
  95.1 3.9 %collective-permute-start.26 = (bf16[128,640]{1,0:T(8,128)(2,1)S(1)}, bf16[128,640]{1,0:T(8,128)(2,1)S(1)}, u32[]{:S(2)}, u32[]{:S(2)}) collective-permute-start(bf16[128,640]{1,0:T(8,128)(2,1)S(1)} %get-tuple-element.105), channel_id=1, source_target_pairs={{0,6},{1,7},{2,4},{3,5},{4,2},{5,3},{6,0},{7,1},{8,14},{9,15},{10,... | collective-permute-start | bytes 491528 | tf_op jit(solution)/shard_map/ppermute | solution.py:32
  101.7 2.9 %collective-permute-start.25 = (bf16[128,640]{1,0:T(8,128)(2,1)S(1)}, bf16[128,640]{1,0:T(8,128)(2,1)S(1)}, u32[]{:S(2)}, u32[]{:S(2)}) collective-permute-start(bf16[128,640]{1,0:T(8,128)(2,1)S(1)} %get-tuple-element.116), channel_id=1, source_target_pairs={{0,3},{1,2},{2,1},{3,0},{4,7},{5,6},{6,5},{7,4},{8,11},{9,10},{10,... | collective-permute-start | bytes 491528 | tf_op jit(solution)/shard_map/ppermute | solution.py:32
  108.9 2.7 %collective-permute-start.15 = (bf16[128,640]{1,0:T(8,128)(2,1)S(1)}, bf16[128,640]{1,0:T(8,128)(2,1)S(1)}, u32[]{:S(2)}, u32[]{:S(2)}) collective-permute-start(bf16[128,640]{1,0:T(8,128)(2,1)S(1)} %get-tuple-element.96), channel_id=1, source_target_pairs={{0,5},{1,4},{2,7},{3,6},{4,1},{5,0},{6,3},{7,2},{8,13},{9,12},{10,... | collective-permute-start | bytes 491528 | tf_op jit(solution)/shard_map/ppermute | solution.py:32
  111.7 2.7 %collective-permute-done.25 = bf16[128,640]{1,0:T(8,128)(2,1)S(1)} collective-permute-done((bf16[128,640]{1,0:T(8,128)(2,1)S(1)}, bf16[128,640]{1,0:T(8,128)(2,1)S(1)}, u32[]{:S(2)}, u32[]{:S(2)}) %collective-permute-start.25) | collective-permute-done | bytes 163872 | tf_op jit(solution)/shard_map/ppermute | solution.py:32
  116.9 3.5 %collective-permute-done.15 = bf16[128,640]{1,0:T(8,128)(2,1)S(1)} collective-permute-done((bf16[128,640]{1,0:T(8,128)(2,1)S(1)}, bf16[128,640]{1,0:T(8,128)(2,1)S(1)}, u32[]{:S(2)}, u32[]{:S(2)}) %collective-permute-start.15) | collective-permute-done | bytes 163872 | tf_op jit(solution)/shard_map/ppermute | solution.py:32
  127.1 3.5 %shard_map.134 = (bf16[512,640]{1,0:T(8,128)(2,1)}, bf16[512,640]{1,0:T(8,128)(2,1)S(1)}) custom-call(s32[2]{0:T(128)S(1)} %pad_add_fusion.where_ref, f32[2048,8]{1,0:T(8,128)S(1)} %get-tuple-element.66.place_ref, f32[1024,640]{1,0:T(8,128)S(1)} %shard_map.133.base_ref, bf16[256,640]{1,0:T(8,128)(2,1)S(1)} %collective-permute-done.28.refs_0_, ...), custom_call_target="tpu_custom_call" | custom-call | flops 3019898880 | bytes 14745600 | tf_op jit(solution)/shard_map/pallas_call | solution.py:19
  131.7 16.0 %collective-permute-done.31.refs_1_ = bf16[512,640]{1,0:T(8,128)(2,1)} collective-permute-done((bf16[512,640]{1,0:T(8,128)(2,1)}, bf16[512,640]{1,0:T(8,128)(2,1)}, u32[]{:S(2)}, u32[]{:S(2)}) %collective-permute-start.31) | collective-permute-done | bytes 655392 | tf_op jit(solution)/shard_map/ppermute | solution.py:32
  149.0 5.9 %shard_map.135 = (bf16[3,320,2048]{2,1,0:T(8,128)(2,1)}, bf16[512,1280]{1,0:T(8,128)(2,1)}) custom-call(s32[2]{0:T(128)S(1)} %pad_add_fusion.5.where_ref, f32[1,1280]{1,0:T(1,128)S(1)} %broadcast_in_dim.6.gain_ref, bf16[960,1280]{1,0:T(8,128)(2,1)} %bitcast.51, bf16[512,640]{1,0:T(8,128)(2,1)} %get-tuple-element.122.refs_0_, ...), custom_call_target="tpu_custom_call" | custom-call | flops 1258291200 | bytes 4751360 | tf_op jit(solution)/shard_map/pallas_call | solution.py:395
  154.9 5.2 %shard_map.136.refs_2_ = bf16[3,320,2048]{2,1,0:T(8,128)(2,1)} custom-call(s32[2]{0:T(128)S(1)} %pad_add_fusion.2.where_ref, f32[1,1280]{1,0:T(1,128)S(1)} %broadcast_in_dim.6.gain_ref, bf16[960,1280]{1,0:T(8,128)(2,1)} %bitcast.52, bf16[512,640]{1,0:T(8,128)(2,1)S(1)} %collective-permute-done.33.refs_0_, ...), custom_call_target="tpu_custom_call", output_to_operand_aliasing={{}: (5, {})} | custom-call | flops 1258291200 | bytes 4751360 | tf_op jit(solution)/shard_map/pallas_call | solution.py:395
  160.2 4.6 %collective-permute-done.32.refs_1_ = bf16[512,640]{1,0:T(8,128)(2,1)S(1)} collective-permute-done((bf16[512,640]{1,0:T(8,128)(2,1)S(1)}, bf16[512,640]{1,0:T(8,128)(2,1)S(1)}, u32[]{:S(2)}, u32[]{:S(2)}) %collective-permute-start.32) | collective-permute-done | bytes 655392 | tf_op jit(solution)/shard_map/ppermute | solution.py:32
  165.5 4.6 %shard_map.137 = (bf16[3,320,2048]{2,1,0:T(8,128)(2,1)}, bf16[512,1280]{1,0:T(8,128)(2,1)}) custom-call(s32[2]{0:T(128)S(1)} %pad_add_fusion.4.where_ref, f32[1,1280]{1,0:T(1,128)S(1)} %broadcast_in_dim.6.gain_ref, bf16[960,1280]{1,0:T(8,128)(2,1)} %bitcast.53, ...), custom_call_target="tpu_custom_call", output_to_operand_aliasing={{0}: (5, {}), {1}: (6, {})} | custom-call | flops 1258291200 | bytes 4751360 | tf_op jit(solution)/shard_map/pallas_call | solution.py:395
  170.1 5.2 %shard_map.138 = bf16[3,320,2048]{2,1,0:T(8,128)(2,1)} custom-call(s32[2]{0:T(128)S(1)} %pad_add_fusion.3.where_ref, f32[1,1280]{1,0:T(1,128)S(1)} %broadcast_in_dim.6.gain_ref, bf16[960,1280]{1,0:T(8,128)(2,1)} %bitcast.54, bf16[512,640]{1,0:T(8,128)(2,1)S(1)} %collective-permute-done.35.refs_0_, ...), custom_call_target="tpu_custom_call", output_to_operand_aliasing={{}: (5, {})} | custom-call | flops 1258291200 | bytes 4751360 | tf_op jit(solution)/shard_map/pallas_call | solution.py:395
  (115 shorter events, 38.9 us)
Async XLA Ops:
  0.7 21.6 %collective-permute-start.3 = (bf16[1280,1280]{1,0:T(8,128)(2,1)}, bf16[1280,1280]{1,0:T(8,128)(2,1)}, u32[]{:S(2)}, u32[]{:S(2)}) collective-permute-start(bf16[1280,1280]{1,0:T(8,128)(2,1)} %bitcast.40), channel_id=1, source_target_pairs={{0,8},{8,0},{16,24},{24,16},{1,9},{9,1},{17,25},{25,17},{2,10},{10... | collective-permute-start | bytes 9830408 | tf_op jit(solution)/shard_map/ppermute | solution.py:32
  1.2 21.1 %collective-permute-start.4 = (bf16[1280,1280]{1,0:T(8,128)(2,1)}, bf16[1280,1280]{1,0:T(8,128)(2,1)}, u32[]{:S(2)}, u32[]{:S(2)}) collective-permute-start(bf16[1280,1280]{1,0:T(8,128)(2,1)} %bitcast.45), channel_id=1, source_target_pairs={{0,8},{8,0},{16,24},{24,16},{1,9},{9,1},{17,25},{25,17},{2,10},{10... | collective-permute-start | bytes 9830408 | tf_op jit(solution)/shard_map/ppermute | solution.py:32
  2.0 17.8 %collective-permute-start = (bf16[512,640]{1,0:T(8,128)(2,1)S(1)}, bf16[512,640]{1,0:T(8,128)(2,1)}, u32[]{:S(2)}, u32[]{:S(2)}) collective-permute-start(bf16[512,640]{1,0:T(8,128)(2,1)S(1)} %constant_dynamic-slice_fusion.1), channel_id=1, source_target_pairs={{0,16},{8,24},{16,0},{24,8},{1,17},{9,25},{17,1},{25,9},{2,18},{10... | collective-permute-start | bytes 1966088 | tf_op jit(solution)/shard_map/ppermute | solution.py:32
  5.1 15.9 %collective-permute-start.1 = (bf16[512,640]{1,0:T(8,128)(2,1)S(1)}, bf16[512,640]{1,0:T(8,128)(2,1)}, u32[]{:S(2)}, u32[]{:S(2)}) collective-permute-start(bf16[512,640]{1,0:T(8,128)(2,1)S(1)} %constant_dynamic-slice_fusion.refs_0_), channel_id=1, source_target_pairs={{0,8},{8,0},{16,24},{24,16},{1,9},{9,1},{17,25},{25,17},{2,10},{10... | collective-permute-start | bytes 1966088 | tf_op jit(solution)/shard_map/ppermute | solution.py:32
  31.8 13.8 %collective-permute-start.8 = (bf16[128,640]{1,0:T(8,128)(2,1)S(1)}, bf16[128,640]{1,0:T(8,128)(2,1)S(1)}, u32[]{:S(2)}, u32[]{:S(2)}) collective-permute-start(bf16[128,640]{1,0:T(8,128)(2,1)S(1)} %get-tuple-element.77), channel_id=1, source_target_pairs={{0,2},{1,3},{2,0},{3,1},{4,6},{5,7},{6,4},{7,5},{8,10},{9,11},{10,... | collective-permute-start | bytes 491528 | tf_op jit(solution)/shard_map/ppermute | solution.py:32
  33.4 13.4 %collective-permute-start.9 = (bf16[128,640]{1,0:T(8,128)(2,1)S(1)}, bf16[128,640]{1,0:T(8,128)(2,1)S(1)}, u32[]{:S(2)}, u32[]{:S(2)}) collective-permute-start(bf16[128,640]{1,0:T(8,128)(2,1)S(1)} %get-tuple-element.78), channel_id=1, source_target_pairs={{0,3},{1,2},{2,1},{3,0},{4,7},{5,6},{6,5},{7,4},{8,11},{9,10},{10,... | collective-permute-start | bytes 491528 | tf_op jit(solution)/shard_map/ppermute | solution.py:32
  33.6 14.9 %collective-permute-start.5 = (bf16[128,640]{1,0:T(8,128)(2,1)S(1)}, bf16[128,640]{1,0:T(8,128)(2,1)S(1)}, u32[]{:S(2)}, u32[]{:S(2)}) collective-permute-start(bf16[128,640]{1,0:T(8,128)(2,1)S(1)} %get-tuple-element.75), channel_id=1, source_target_pairs={{0,4},{1,5},{2,6},{3,7},{4,0},{5,1},{6,2},{7,3},{8,12},{9,13},{10,... | collective-permute-start | bytes 491528 | tf_op jit(solution)/shard_map/ppermute | solution.py:32
  36.5 15.2 %collective-permute-start.6 = (bf16[128,640]{1,0:T(8,128)(2,1)S(1)}, bf16[128,640]{1,0:T(8,128)(2,1)S(1)}, u32[]{:S(2)}, u32[]{:S(2)}) collective-permute-start(bf16[128,640]{1,0:T(8,128)(2,1)S(1)} %get-tuple-element.76), channel_id=1, source_target_pairs={{0,5},{1,4},{2,7},{3,6},{4,1},{5,0},{6,3},{7,2},{8,13},{9,12},{10,... | collective-permute-start | bytes 491528 | tf_op jit(solution)/shard_map/ppermute | solution.py:32
  37.8 15.5 %collective-permute-start.12 = (bf16[256,640]{1,0:T(8,128)(2,1)S(1)}, bf16[256,640]{1,0:T(8,128)(2,1)S(1)}, u32[]{:S(2)}, u32[]{:S(2)}) collective-permute-start(bf16[256,640]{1,0:T(8,128)(2,1)S(1)} %constant_dynamic-update-slice_fusion.4.refs_0_), channel_id=1, source_target_pairs={{0,16},{8,24},{16,0},{24,8},{1,17},{9,25},{17,1},{25,9},{2,18},{10... | collective-permute-start | bytes 983048 | tf_op jit(solution)/shard_map/ppermute | solution.py:32
  46.8 16.7 %collective-permute-start.10 = (bf16[256,640]{1,0:T(8,128)(2,1)S(1)}, bf16[256,640]{1,0:T(8,128)(2,1)S(1)}, u32[]{:S(2)}, u32[]{:S(2)}) collective-permute-start(bf16[256,640]{1,0:T(8,128)(2,1)S(1)} %constant_dynamic-update-slice_fusion.2.refs_0_), channel_id=1, source_target_pairs={{0,16},{8,24},{16,0},{24,8},{1,17},{9,25},{17,1},{25,9},{2,18},{10... | collective-permute-start | bytes 983048 | tf_op jit(solution)/shard_map/ppermute | solution.py:32
  51.7 18.0 %collective-permute-start.7 = (bf16[256,640]{1,0:T(8,128)(2,1)S(1)}, bf16[256,640]{1,0:T(8,128)(2,1)S(1)}, u32[]{:S(2)}, u32[]{:S(2)}) collective-permute-start(bf16[256,640]{1,0:T(8,128)(2,1)S(1)} %constant_dynamic-update-slice_fusion.refs_0_), channel_id=1, source_target_pairs={{0,16},{8,24},{16,0},{24,8},{1,17},{9,25},{17,1},{25,9},{2,18},{10... | collective-permute-start | bytes 983048 | tf_op jit(solution)/shard_map/ppermute | solution.py:32
  53.3 16.5 %collective-permute-start.16 = (bf16[128,640]{1,0:T(8,128)(2,1)S(1)}, bf16[128,640]{1,0:T(8,128)(2,1)S(1)}, u32[]{:S(2)}, u32[]{:S(2)}) collective-permute-start(bf16[128,640]{1,0:T(8,128)(2,1)S(1)} %get-tuple-element.99), channel_id=1, source_target_pairs={{0,6},{1,7},{2,4},{3,5},{4,2},{5,3},{6,0},{7,1},{8,14},{9,15},{10,... | collective-permute-start | bytes 491528 | tf_op jit(solution)/shard_map/ppermute | solution.py:32
  57.6 12.2 %collective-permute-start.17 = (bf16[128,640]{1,0:T(8,128)(2,1)S(1)}, bf16[128,640]{1,0:T(8,128)(2,1)S(1)}, u32[]{:S(2)}, u32[]{:S(2)}) collective-permute-start(bf16[128,640]{1,0:T(8,128)(2,1)S(1)} %get-tuple-element.100), channel_id=1, source_target_pairs={{0,7},{1,6},{2,5},{3,4},{4,3},{5,2},{6,1},{7,0},{8,15},{9,14},{10,... | collective-permute-start | bytes 491528 | tf_op jit(solution)/shard_map/ppermute | solution.py:32
  84.2 10.7 %collective-permute-start.19 = (bf16[256,640]{1,0:T(8,128)(2,1)S(1)}, bf16[256,640]{1,0:T(8,128)(2,1)S(1)}, u32[]{:S(2)}, u32[]{:S(2)}) collective-permute-start(bf16[256,640]{1,0:T(8,128)(2,1)S(1)} %get-tuple-element.104), channel_id=1, source_target_pairs={{0,16},{8,24},{16,0},{24,8},{1,17},{9,25},{17,1},{25,9},{2,18},{10... | collective-permute-start | bytes 983048 | tf_op jit(solution)/shard_map/ppermute | solution.py:32
  84.6 17.0 %collective-permute-start.23 = (bf16[256,640]{1,0:T(8,128)(2,1)S(1)}, bf16[256,640]{1,0:T(8,128)(2,1)S(1)}, u32[]{:S(2)}, u32[]{:S(2)}) collective-permute-start(bf16[256,640]{1,0:T(8,128)(2,1)S(1)} %get-tuple-element.114), channel_id=1, source_target_pairs={{0,16},{8,24},{16,0},{24,8},{1,17},{9,25},{17,1},{25,9},{2,18},{10... | collective-permute-start | bytes 983048 | tf_op jit(solution)/shard_map/ppermute | solution.py:32
  95.0 16.7 %collective-permute-start.20 = (bf16[256,640]{1,0:T(8,128)(2,1)S(1)}, bf16[256,640]{1,0:T(8,128)(2,1)S(1)}, u32[]{:S(2)}, u32[]{:S(2)}) collective-permute-start(bf16[256,640]{1,0:T(8,128)(2,1)S(1)} %get-tuple-element.107), channel_id=1, source_target_pairs={{0,16},{8,24},{16,0},{24,8},{1,17},{9,25},{17,1},{25,9},{2,18},{10... | collective-permute-start | bytes 983048 | tf_op jit(solution)/shard_map/ppermute | solution.py:32
  99.0 9.9 %collective-permute-start.27 = (bf16[128,640]{1,0:T(8,128)(2,1)S(1)}, bf16[128,640]{1,0:T(8,128)(2,1)S(1)}, u32[]{:S(2)}, u32[]{:S(2)}) collective-permute-start(bf16[128,640]{1,0:T(8,128)(2,1)S(1)} %get-tuple-element.106), channel_id=1, source_target_pairs={{0,7},{1,6},{2,5},{3,4},{4,3},{5,2},{6,1},{7,0},{8,15},{9,14},{10,... | collective-permute-start | bytes 491528 | tf_op jit(solution)/shard_map/ppermute | solution.py:32
  101.6 10.0 %collective-permute-start.24 = (bf16[128,640]{1,0:T(8,128)(2,1)S(1)}, bf16[128,640]{1,0:T(8,128)(2,1)S(1)}, u32[]{:S(2)}, u32[]{:S(2)}) collective-permute-start(bf16[128,640]{1,0:T(8,128)(2,1)S(1)} %get-tuple-element.115), channel_id=1, source_target_pairs={{0,2},{1,3},{2,0},{3,1},{4,6},{5,7},{6,4},{7,5},{8,10},{9,11},{10,... | collective-permute-start | bytes 491528 | tf_op jit(solution)/shard_map/ppermute | solution.py:32
  101.7 12.6 %collective-permute-start.25 = (bf16[128,640]{1,0:T(8,128)(2,1)S(1)}, bf16[128,640]{1,0:T(8,128)(2,1)S(1)}, u32[]{:S(2)}, u32[]{:S(2)}) collective-permute-start(bf16[128,640]{1,0:T(8,128)(2,1)S(1)} %get-tuple-element.116), channel_id=1, source_target_pairs={{0,3},{1,2},{2,1},{3,0},{4,7},{5,6},{6,5},{7,4},{8,11},{9,10},{10,... | collective-permute-start | bytes 491528 | tf_op jit(solution)/shard_map/ppermute | solution.py:32
  104.7 12.2 %collective-permute-start.14 = (bf16[128,640]{1,0:T(8,128)(2,1)S(1)}, bf16[128,640]{1,0:T(8,128)(2,1)S(1)}, u32[]{:S(2)}, u32[]{:S(2)}) collective-permute-start(bf16[128,640]{1,0:T(8,128)(2,1)S(1)} %get-tuple-element.95), channel_id=1, source_target_pairs={{0,4},{1,5},{2,6},{3,7},{4,0},{5,1},{6,2},{7,3},{8,12},{9,13},{10,... | collective-permute-start | bytes 491528 | tf_op jit(solution)/shard_map/ppermute | solution.py:32
  108.9 11.5 %collective-permute-start.15 = (bf16[128,640]{1,0:T(8,128)(2,1)S(1)}, bf16[128,640]{1,0:T(8,128)(2,1)S(1)}, u32[]{:S(2)}, u32[]{:S(2)}) collective-permute-start(bf16[128,640]{1,0:T(8,128)(2,1)S(1)} %get-tuple-element.96), channel_id=1, source_target_pairs={{0,5},{1,4},{2,7},{3,6},{4,1},{5,0},{6,3},{7,2},{8,13},{9,12},{10,... | collective-permute-start | bytes 491528 | tf_op jit(solution)/shard_map/ppermute | solution.py:32
  130.6 17.1 %collective-permute-start.31 = (bf16[512,640]{1,0:T(8,128)(2,1)}, bf16[512,640]{1,0:T(8,128)(2,1)}, u32[]{:S(2)}, u32[]{:S(2)}) collective-permute-start(bf16[512,640]{1,0:T(8,128)(2,1)} %get-tuple-element.122.refs_0_), channel_id=1, source_target_pairs={{0,16},{8,24},{16,0},{24,8},{1,17},{9,25},{17,1},{25,9},{2,18},{10... | collective-permute-start | bytes 1966088 | tf_op jit(solution)/shard_map/ppermute | solution.py:32
  131.5 23.4 %collective-permute-start.33 = (bf16[512,640]{1,0:T(8,128)(2,1)}, bf16[512,640]{1,0:T(8,128)(2,1)S(1)}, u32[]{:S(2)}, u32[]{:S(2)}) collective-permute-start(bf16[512,640]{1,0:T(8,128)(2,1)} %get-tuple-element.122.refs_0_), channel_id=1, source_target_pairs={{0,8},{8,0},{16,24},{24,16},{1,9},{9,1},{17,25},{25,17},{2,10},{10... | collective-permute-start | bytes 1966088 | tf_op jit(solution)/shard_map/ppermute | solution.py:32
  147.7 17.1 %collective-permute-start.32 = (bf16[512,640]{1,0:T(8,128)(2,1)S(1)}, bf16[512,640]{1,0:T(8,128)(2,1)S(1)}, u32[]{:S(2)}, u32[]{:S(2)}) collective-permute-start(bf16[512,640]{1,0:T(8,128)(2,1)S(1)} %get-tuple-element.125.refs_0_), channel_id=1, source_target_pairs={{0,16},{8,24},{16,0},{24,8},{1,17},{9,25},{17,1},{25,9},{2,18},{10... | collective-permute-start | bytes 1966088 | tf_op jit(solution)/shard_map/ppermute | solution.py:32
  (23 other events, 281.6 us)
where the time goes:
time: 176 us
  waiting for transfers between devices  68.1 us (39%)
  Pallas kernels  62.4 us (35%)
  starting transfers between devices  42.1 us (24%)
    ppermute x37, waiting for transfers between devices, swap(): return lax.ppermute(value, axis, [(i, i ^ distance) for i in range(count)])  68.1 us
    ppermute x37, starting transfers between devices, swap(): return lax.ppermute(value, axis, [(i, i ^ distance) for i in range(count)])  42.1 us
    pallas_call x13, Pallas kernels, call(): pl.pallas_call(kernel, out_shape=out_shape, in_specs=in_specs, out_specs=...  41.5 us
    pallas_call x4, Pallas kernels, qkv_project(): pl.pallas_call(functools.partial(qkv_kernel, shares, block, len(earlier))...  20.9 us
  transfers between devices with their start and end apart: 37, of which 15 were waited for; matrix products, arithmetic and copies ran while one was open for 1% of the time, Pallas kernels for 26%

commit v1 on v0

--- a/solution.py
+++ b/solution.py
@@ -267,48 +267,32 @@
     )
 
 
-def combine_kernel(firsts, blocks, where_ref, place_ref, base_ref, *refs):
-    sources, outs = refs[: len(firsts)], refs[len(firsts) :]
+def combine_kernel(firsts, skipped, where_ref, place_ref, base_ref, *refs):
+    sources, out = refs[: len(firsts)], refs[len(firsts)]
     choices = 2
-    rows = base_ref.shape[0] // blocks
-
-    def add(i):
-        at = pl.ds(i * rows if isinstance(i, int) else pl.multiple_of(i * rows, rows), rows)
-        start = pl.multiple_of(where_ref[i] * rows, rows)
-        table = place_ref[pl.ds(start, rows)]
-        place, gate = table[:, :choices].astype(jnp.int32), table[:, choices : 2 * choices]
-        total = base_ref[at].astype(f32)
-        for first, source in zip(firsts, sources):
-            many = source.shape[0]
-            lanes = lax.broadcasted_iota(jnp.int32, (rows, many), 1) + first
-            weight = jnp.zeros((rows, many), f32)
-            for k in range(choices):
-                weight = jnp.where(lanes == place[:, k : k + 1], gate[:, k : k + 1], weight)
-            total = total + jnp.dot(weight.astype(bf16), source[...], preferred_element_type=f32)
-        if len(outs) == 1:
-            outs[0][at] = total
-        else:
-            outs[i][...] = total.astype(bf16)
-
-    if len(outs) == 1:
-        lax.fori_loop(0, blocks, lambda i, carry: (add(i), carry)[1], 0)
-    else:
-        for i in range(blocks):
-            add(i)
-
-
-def combine(where, places, base, sources, firsts, last):
-    blocks = where.shape[0]
-    rows, cols = base.shape
+    rows = out.shape[0]
+    start = pl.multiple_of(where_ref[0] * rows, rows)
+    table = place_ref[pl.ds(start, rows)]
+    place, gate = table[:, :choices].astype(jnp.int32), table[:, choices : 2 * choices]
+    total = base_ref[skipped : skipped + rows].astype(f32)
+    for first, source in zip(firsts, sources):
+        many = source.shape[0]
+        lanes = lax.broadcasted_iota(jnp.int32, (rows, many), 1) + first
+        weight = jnp.zeros((rows, many), f32)
+        for k in range(choices):
+            weight = jnp.where(lanes == place[:, k : k + 1], gate[:, k : k + 1], weight)
+        total = total + jnp.dot(weight.astype(bf16), source[...], preferred_element_type=f32)
+    out[...] = total.astype(out.dtype)
+
+
+def combine(where, places, base, sources, firsts, rows, skipped, dtype):
+    cols = base.shape[1]
     many = sum(source.shape[0] for source in sources)
-    shapes = [jax.ShapeDtypeStruct((rows, cols), f32)]
-    if last:
-        shapes = [jax.ShapeDtypeStruct((rows // blocks, cols), bf16)] * blocks
     return call(
-        functools.partial(combine_kernel, firsts, blocks),
-        shapes,
+        functools.partial(combine_kernel, firsts, skipped),
+        jax.ShapeDtypeStruct((rows, cols), dtype),
         [SMEM, VMEM, VMEM] + [VMEM] * len(sources),
-        [VMEM] * len(shapes),
+        VMEM,
         [],
         20,
         2 * rows * many * cols,
@@ -320,7 +304,7 @@
     )
 
 
-def qkv_kernel(shares, block, earlier, where_ref, gain_ref, weight_ref, *refs):
+def qkv_kernel(shares, block, quick, earlier, where_ref, gain_ref, weight_ref, *refs):
     parts, refs = refs[:shares], refs[shares + earlier :]
     out, refs = refs[0], refs[1:]
     if block is not None:
@@ -353,17 +337,32 @@
                     stage[:, pl.ds(start, cols)] = part[...]
                 pltpu.make_async_copy(stage, stream, stage_sem).start()
 
-        for left in range(0, rows, tile):
-            at = slice(left, left + tile)
+        def norm(at):
             normalise([part[at] for part in parts], starts, gain_ref, normed.at[at])
-        for load in loads:
-            load.wait()
-        for left in range(0, rows, tile):
-            at = slice(left, left + tile)
+
+        def project(at):
             result = lax.dot_general(
                 weights[...], normed[at], (((1,), (1,)), ((), ())), preferred_element_type=f32
             )
             held[:, at] = result.astype(bf16)
+
+        def step(t, carry):
+            at = pl.ds(pl.multiple_of(t * tile, tile), tile)
+            norm(at)
+            project(at)
+            return carry
+
+        tiles = [slice(left, left + tile) for left in range(0, rows, tile)]
+        if quick:
+            for at in tiles:
+                norm(at)
+        for load in loads:
+            load.wait()
+        if quick:
+            for at in tiles:
+                project(at)
+        else:
+            lax.fori_loop(0, rows // tile, step, 0)
         for copy in copies:
             copy.start()
 
@@ -377,7 +376,7 @@
             pltpu.make_async_copy(stage, stream, stage_sem).wait()
 
 
-def qkv_project(where, gain, weight, parts, total, block, earlier):
+def qkv_project(where, gain, weight, parts, total, block, quick, earlier):
     shares = len(parts)
     rows = parts[0].shape[0]
     wide, width = weight.shape
@@ -393,7 +392,7 @@
         shapes += [jax.ShapeDtypeStruct((rows, width), bf16)]
         scratch += [pltpu.VMEM((rows, width), bf16), pltpu.SemaphoreType.DMA]
     return pl.pallas_call(
-        functools.partial(qkv_kernel, shares, block, len(earlier)),
+        functools.partial(qkv_kernel, shares, block, quick, len(earlier)),
         out_shape=shapes,
         in_specs=[SMEM, VMEM, pl.BlockSpec(memory_space=pltpu.HBM)]
         + [VMEM] * shares
@@ -510,36 +509,55 @@
         returned[g] = [
             swap(block, "expert", k) if k else block for k, block in zip(groups[g], sent_back[g])
         ]
-    for g in (1, 2, 3):
-        returned[g] = after(returned[g], *received[0])
+    returned = after(returned, *received[0], *received[1])
     back = [jnp.concatenate(blocks, 0) for blocks in returned]
     over_back = [swap(value, "tm", 1) for value in back]
-    total = base
-    steps = [[(2, 0), (2, 1)], [(0, 0), (1, 0), (3, 0)], [(0, 1), (1, 1), (3, 1)]]
-    for step in steps:
-        sources = [(over_back if side else back)[g] for g, side in step]
-        firsts = [(side * experts + groups[g].start) * half for g, side in step]
-        done = combine(blocks_here, back_place, total, sources, firsts, step is steps[-1])
-        total = done[0]
-    stream = list(done)
+    tables = [(g, side) for side in range(2) for g in range(len(groups))]
+    first_steps = [[(2, 0), (2, 1)], [(0, 0), (1, 0), (3, 0)], [(0, 1), (1, 1), (3, 1)]]
+    stream = []
+    for i in range(chips):
+        total, skipped = base, i * own_rows
+        steps = [tables] if i else first_steps
+        for step in steps:
+            sources = [(over_back if side else back)[g] for g, side in step]
+            firsts = [(side * experts + groups[g].start) * half for g, side in step]
+            total = combine(
+                blocks_here[i : i + 1],
+                back_place,
+                total,
+                sources,
+                firsts,
+                own_rows,
+                skipped,
+                bf16 if step is steps[-1] else f32,
+            )
+            skipped = 0
+        stream.append(total)
+
     qkv_rows, own_stream, before = [], [], None
     for i in range(chips):
         if before:
             stream[i] = after(stream[i], *before)
         pieces = [stream[i]] + [swap(stream[i], "tm", 2 * d) for d in range(1, chips)]
         before = pieces
+        if i < chips - 1:
+            pieces = after(pieces, stream[i + 1])
         if i:
             pieces = after(pieces, *qkv_rows)
         other = [swap(piece, "tm", 1) for piece in pieces]
-        where = jnp.stack([chip, 2 * i + core]).astype(jnp.int32)
-        *qkv_rows, own = qkv_project(
-            where, attn_gain[None], qkv_columns, pieces, rows, i, qkv_rows + own_stream
-        )
-        own_stream = [own]
-        where = jnp.stack([chip, 2 * i + 1 - core]).astype(jnp.int32)
-        qkv_rows = list(
-            qkv_project(where, attn_gain[None], qkv_columns, other, rows, None, qkv_rows)
-        )
+        for side, parts in ((core, pieces), (1 - core, other)):
+            own = parts is pieces
+            done = qkv_project(
+                jnp.stack([chip, 2 * i + side]).astype(jnp.int32),
+                attn_gain[None],
+                qkv_columns,
+                parts,
+                rows,
+                i if own else None,
+                i == chips - 1,
+                qkv_rows + (own_stream if own else []),
+            )
+            qkv_rows, own_stream = [done[0]], [done[1]] if own else own_stream
     return (own_stream[0].reshape(tokens.shape), jnp.swapaxes(qkv_rows[0], 1, 2)[:, None])
 
 

time: 176 us -> 174 us (0.989)
  waiting for transfers between devices: 68.1 us -> 61.4 us
  starting transfers between devices: 42.1 us -> 45.5 us
    ppermute x37, waiting for transfers between devices: 68.1 us -> 61.4 us  [swap(): return lax.ppermute(value, axis, [(i, i ^ distance) for i in range(count)])]
    ppermute x37, starting transfers between devices: 42.1 us -> 45.5 us  [swap(): return lax.ppermute(value, axis, [(i, i ^ distance) for i in range(count)])]
    pallas_call x4, Pallas kernels: 20.9 us -> 23.9 us  [qkv_project(): pl.pallas_call(functools.partial(qkv_kernel, shares, block, quick, len(ea...]
    pallas_call x13 -> x14, Pallas kernels: 41.5 us -> 39 us  [call(): pl.pallas_call(kernel, out_shape=out_shape, in_specs=in_specs, out_specs=...]
  transfers between devices with their start and end apart: 37 -> 37, of which waited for: 15 -> 15; matrix products, arithmetic and copies ran while one was open for 1% -> 0% of each run, Pallas kernels for 26% -> 28%
where the time goes in v1:
time: 174 us; the launch traced here: 173 us
  Pallas kernels  62.9 us (36%)
  waiting for transfers between devices  61.4 us (35%)
  starting transfers between devices  45.5 us (26%)
    ppermute x37, waiting for transfers between devices, swap(): return lax.ppermute(value, axis, [(i, i ^ distance) for i in range(count)])  61.4 us
    ppermute x37, starting transfers between devices, swap(): return lax.ppermute(value, axis, [(i, i ^ distance) for i in range(count)])  45.5 us
    pallas_call x14, Pallas kernels, call(): pl.pallas_call(kernel, out_shape=out_shape, in_specs=in_specs, out_specs=...  39 us
    pallas_call x4, Pallas kernels, qkv_project(): pl.pallas_call(functools.partial(qkv_kernel, shares, block, quick, len(ea...  23.9 us
  transfers between devices with their start and end apart: 37, of which 15 were waited for; matrix products, arithmetic and copies ran while one was open for 0% of the time, Pallas kernels for 28%

profile of v1, /device:TPU:0, one launch (start us, length us, event | category | flops | bytes accessed | tf_op | source)
XLA Modules:
  0.0 172.6 jit_solution(8180090753529928197)
XLA Ops:
  2.0 3.0 %collective-permute-start = (bf16[512,640]{1,0:T(8,128)(2,1)S(1)}, bf16[512,640]{1,0:T(8,128)(2,1)}, u32[]{:S(2)}, u32[]{:S(2)}) collective-permute-start(bf16[512,640]{1,0:T(8,128)(2,1)S(1)} %constant_dynamic-slice_fusion.1), channel_id=1, source_target_pairs={{0,16},{8,24},{16,0},{24,8},{1,17},{9,25},{17,1},{25,9},{2,18},{10... | collective-permute-start | bytes 1966088 | tf_op jit(solution)/shard_map/ppermute | solution.py:32
  5.2 14.7 %collective-permute-done.refs_1_ = bf16[512,640]{1,0:T(8,128)(2,1)} collective-permute-done((bf16[512,640]{1,0:T(8,128)(2,1)S(1)}, bf16[512,640]{1,0:T(8,128)(2,1)}, u32[]{:S(2)}, u32[]{:S(2)}) %collective-permute-start) | collective-permute-done | bytes 655392 | tf_op jit(solution)/shard_map/ppermute | solution.py:32
  22.3 7.6 %shard_map.123 = (bf16[1024,640]{1,0:T(8,128)(2,1)S(1)}, bf16[128,640]{1,0:T(8,128)(2,1)S(1)}, bf16[128,640]{1,0:T(8,128)(2,1)S(1)}, bf16[128,640]{1,0:T(8,128)(...) custom-call(s32[6]{0:T(128)S(1)} %concatenate.27.where_ref, ...), custom_call_target="tpu_custom_call" | custom-call | flops 8053063680 | bytes 11796480 | tf_op jit(solution)/shard_map/pallas_call | solution.py:19
  33.5 2.9 %collective-permute-start.10 = (bf16[128,640]{1,0:T(8,128)(2,1)S(1)}, bf16[128,640]{1,0:T(8,128)(2,1)S(1)}, u32[]{:S(2)}, u32[]{:S(2)}) collective-permute-start(bf16[128,640]{1,0:T(8,128)(2,1)S(1)} %get-tuple-element.89), channel_id=1, source_target_pairs={{0,4},{1,5},{2,6},{3,7},{4,0},{5,1},{6,2},{7,3},{8,12},{9,13},{10,... | collective-permute-start | bytes 491528 | tf_op jit(solution)/shard_map/ppermute | solution.py:32
  39.3 6.3 %collective-permute-done.13 = bf16[128,640]{1,0:T(8,128)(2,1)S(1)} collective-permute-done((bf16[128,640]{1,0:T(8,128)(2,1)S(1)}, bf16[128,640]{1,0:T(8,128)(2,1)S(1)}, u32[]{:S(2)}, u32[]{:S(2)}) %collective-permute-start.13) | collective-permute-done | bytes 163872 | tf_op jit(solution)/shard_map/ppermute | solution.py:32
  48.6 3.1 %collective-permute-done.11 = bf16[128,640]{1,0:T(8,128)(2,1)S(1)} collective-permute-done((bf16[128,640]{1,0:T(8,128)(2,1)S(1)}, bf16[128,640]{1,0:T(8,128)(2,1)S(1)}, u32[]{:S(2)}, u32[]{:S(2)}) %collective-permute-start.11) | collective-permute-done | bytes 163872 | tf_op jit(solution)/shard_map/ppermute | solution.py:32
  53.3 6.0 %shard_map.124 = (bf16[256,640]{1,0:T(8,128)(2,1)S(1)}, bf16[256,640]{1,0:T(8,128)(2,1)S(1)}) custom-call(s32[1]{0:T(128)} %bitcast.where_ref, f32[1,1280]{1,0:T(1,128)S(1)} %broadcast_in_dim.7.gain_ref, bf16[256,640]{1,0:T(8,128)(2,1)S(1)} %constant_dynamic-update-slice_fusion.refs_0_, bf16[256,640]{1,0:T(8,128)(2,1)S(1)} %collective-permute-done.6.refs_1_, ...), custom_call_target="tpu_custom_call" | custom-call | flops 10066329600 | bytes 43253760 | tf_op jit(solution)/shard_map/pallas_call | solution.py:19
  59.3 3.7 %collective-permute-start.7 = (bf16[128,640]{1,0:T(8,128)(2,1)S(1)}, bf16[128,640]{1,0:T(8,128)(2,1)S(1)}, u32[]{:S(2)}, u32[]{:S(2)}) collective-permute-start(bf16[128,640]{1,0:T(8,128)(2,1)S(1)} %get-tuple-element.87), channel_id=1, source_target_pairs={{0,6},{1,7},{2,4},{3,5},{4,2},{5,3},{6,0},{7,1},{8,14},{9,15},{10,... | collective-permute-start | bytes 491528 | tf_op jit(solution)/shard_map/ppermute | solution.py:32
  63.5 6.1 %shard_map.125 = (bf16[256,640]{1,0:T(8,128)(2,1)S(1)}, bf16[256,640]{1,0:T(8,128)(2,1)S(1)}) custom-call(s32[1]{0:T(128)} %bitcast.where_ref, f32[1,1280]{1,0:T(1,128)S(1)} %broadcast_in_dim.7.gain_ref, bf16[256,640]{1,0:T(8,128)(2,1)S(1)} %constant_dynamic-update-slice_fusion.6.refs_0_, bf16[256,640]{1,0:T(8,128)(2,1)S(1)} %collective-permute-done.15.refs_1_, ...), custom_call_target="tpu_custom_call" | custom-call | flops 10066329600 | bytes 43253760 | tf_op jit(solution)/shard_map/pallas_call | solution.py:19
  71.9 6.0 %shard_map.126 = (bf16[256,640]{1,0:T(8,128)(2,1)S(1)}, bf16[256,640]{1,0:T(8,128)(2,1)S(1)}) custom-call(s32[1]{0:T(128)} %bitcast.where_ref, f32[1,1280]{1,0:T(1,128)S(1)} %broadcast_in_dim.7.gain_ref, bf16[256,640]{1,0:T(8,128)(2,1)S(1)} %constant_dynamic-update-slice_fusion.4.refs_0_, bf16[256,640]{1,0:T(8,128)(2,1)S(1)} %collective-permute-done.12.refs_1_, ...), custom_call_target="tpu_custom_call" | custom-call | flops 10066329600 | bytes 43253760 | tf_op jit(solution)/shard_map/pallas_call | solution.py:19
  79.2 6.2 %shard_map.127 = (bf16[256,640]{1,0:T(8,128)(2,1)S(1)}, bf16[256,640]{1,0:T(8,128)(2,1)S(1)}) custom-call(s32[1]{0:T(128)} %bitcast.where_ref, f32[1,1280]{1,0:T(1,128)S(1)} %broadcast_in_dim.7.gain_ref, bf16[256,640]{1,0:T(8,128)(2,1)S(1)} %constant_dynamic-update-slice_fusion.2.refs_0_, bf16[256,640]{1,0:T(8,128)(2,1)S(1)} %collective-permute-done.9.refs_1_, ...), custom_call_target="tpu_custom_call" | custom-call | flops 10066329600 | bytes 43253760 | tf_op jit(solution)/shard_map/pallas_call | solution.py:19
  87.7 8.5 %collective-permute-done.16.refs_1_ = bf16[256,640]{1,0:T(8,128)(2,1)S(1)} collective-permute-done((bf16[256,640]{1,0:T(8,128)(2,1)S(1)}, bf16[256,640]{1,0:T(8,128)(2,1)S(1)}, u32[]{:S(2)}, u32[]{:S(2)}) %collective-permute-start.16) | collective-permute-done | bytes 327712 | tf_op jit(solution)/shard_map/ppermute | solution.py:32
  98.0 2.5 %collective-permute-start.23 = (bf16[128,640]{1,0:T(8,128)(2,1)S(1)}, bf16[128,640]{1,0:T(8,128)(2,1)S(1)}, u32[]{:S(2)}, u32[]{:S(2)}) collective-permute-start(bf16[128,640]{1,0:T(8,128)(2,1)S(1)} %get-tuple-element.111), channel_id=1, source_target_pairs={{0,4},{1,5},{2,6},{3,7},{4,0},{5,1},{6,2},{7,3},{8,12},{9,13},{10,... | collective-permute-start | bytes 491528 | tf_op jit(solution)/shard_map/ppermute | solution.py:32
  101.0 2.1 %collective-permute-done.20.refs_1_ = bf16[256,640]{1,0:T(8,128)(2,1)S(1)} collective-permute-done((bf16[256,640]{1,0:T(8,128)(2,1)S(1)}, bf16[256,640]{1,0:T(8,128)(2,1)S(1)}, u32[]{:S(2)}, u32[]{:S(2)}) %collective-permute-start.20) | collective-permute-done | bytes 327712 | tf_op jit(solution)/shard_map/ppermute | solution.py:32
  103.3 4.2 %collective-permute-start.21 = (bf16[128,640]{1,0:T(8,128)(2,1)S(1)}, bf16[128,640]{1,0:T(8,128)(2,1)S(1)}, u32[]{:S(2)}, u32[]{:S(2)}) collective-permute-start(bf16[128,640]{1,0:T(8,128)(2,1)S(1)} %get-tuple-element.115), channel_id=1, source_target_pairs={{0,2},{1,3},{2,0},{3,1},{4,6},{5,7},{6,4},{7,5},{8,10},{9,11},{10,... | collective-permute-start | bytes 491528 | tf_op jit(solution)/shard_map/ppermute | solution.py:32
  109.2 3.1 %collective-permute-start.26 = (bf16[128,640]{1,0:T(8,128)(2,1)S(1)}, bf16[128,640]{1,0:T(8,128)(2,1)S(1)}, u32[]{:S(2)}, u32[]{:S(2)}) collective-permute-start(bf16[128,640]{1,0:T(8,128)(2,1)S(1)} %get-tuple-element.106), channel_id=1, source_target_pairs={{0,7},{1,6},{2,5},{3,4},{4,3},{5,2},{6,1},{7,0},{8,15},{9,14},{10,... | collective-permute-start | bytes 491528 | tf_op jit(solution)/shard_map/ppermute | solution.py:32
  112.4 2.4 %collective-permute-done.24 = bf16[128,640]{1,0:T(8,128)(2,1)S(1)} collective-permute-done((bf16[128,640]{1,0:T(8,128)(2,1)S(1)}, bf16[128,640]{1,0:T(8,128)(2,1)S(1)}, u32[]{:S(2)}, u32[]{:S(2)}) %collective-permute-start.24) | collective-permute-done | bytes 163872 | tf_op jit(solution)/shard_map/ppermute | solution.py:32
  117.4 2.8 %collective-permute-done.26 = bf16[128,640]{1,0:T(8,128)(2,1)S(1)} collective-permute-done((bf16[128,640]{1,0:T(8,128)(2,1)S(1)}, bf16[128,640]{1,0:T(8,128)(2,1)S(1)}, u32[]{:S(2)}, u32[]{:S(2)}) %collective-permute-start.26) | collective-permute-done | bytes 163872 | tf_op jit(solution)/shard_map/ppermute | solution.py:32
  128.8 2.1 %shard_map.132.refs_0_ = bf16[512,640]{1,0:T(8,128)(2,1)S(1)} custom-call(s32[1]{0:T(128)} %bitcast.1.where_ref, f32[2048,8]{1,0:T(8,128)S(1)} %get-tuple-element.68.place_ref, bf16[1024,640]{1,0:T(8,128)(2,1)S(1)} %get-tuple-element.76.base_ref, bf16[256,640]{1,0:T(8,128)(2,1)S(1)} %constant_dynamic-update-slice_fusion.8.refs_0_, ...), custom_call_target="tpu_custom_call" | custom-call | flops 4026531840 | bytes 13762560 | tf_op jit(solution)/shard_map/pallas_call | solution.py:19
  130.9 13.6 %collective-permute-done.31.refs_1_ = bf16[512,640]{1,0:T(8,128)(2,1)} collective-permute-done((bf16[512,640]{1,0:T(8,128)(2,1)}, bf16[512,640]{1,0:T(8,128)(2,1)}, u32[]{:S(2)}, u32[]{:S(2)}) %collective-permute-start.31) | collective-permute-done | bytes 655392 | tf_op jit(solution)/shard_map/ppermute | solution.py:32
  146.6 7.2 %shard_map.136 = (bf16[3,320,2048]{2,1,0:T(8,128)(2,1)}, bf16[512,1280]{1,0:T(8,128)(2,1)}) custom-call(s32[2]{0:T(128)S(1)} %pad_add_fusion.4.where_ref, f32[1,1280]{1,0:T(1,128)S(1)} %broadcast_in_dim.6.gain_ref, bf16[960,1280]{1,0:T(8,128)(2,1)} %bitcast.51, bf16[512,640]{1,0:T(8,128)(2,1)} %shard_map.135.refs_0_, ...), custom_call_target="tpu_custom_call" | custom-call | flops 1258291200 | bytes 4751360 | tf_op jit(solution)/shard_map/pallas_call | solution.py:394
  153.8 6.7 %shard_map.137.refs_2_ = bf16[3,320,2048]{2,1,0:T(8,128)(2,1)} custom-call(s32[2]{0:T(128)S(1)} %pad_add_fusion.2.where_ref, f32[1,1280]{1,0:T(1,128)S(1)} %broadcast_in_dim.6.gain_ref, bf16[960,1280]{1,0:T(8,128)(2,1)} %bitcast.52, bf16[512,640]{1,0:T(8,128)(2,1)} %collective-permute-done.33.refs_0_, ...), custom_call_target="tpu_custom_call", output_to_operand_aliasing={{}: (5, {})} | custom-call | flops 1258291200 | bytes 4751360 | tf_op jit(solution)/shard_map/pallas_call | solution.py:394
  162.3 4.6 %shard_map.138 = (bf16[3,320,2048]{2,1,0:T(8,128)(2,1)}, bf16[512,1280]{1,0:T(8,128)(2,1)}) custom-call(s32[2]{0:T(128)S(1)} %pad_add_fusion.where_ref, f32[1,1280]{1,0:T(1,128)S(1)} %broadcast_in_dim.6.gain_ref, bf16[960,1280]{1,0:T(8,128)(2,1)} %bitcast.53, bf16[512,640]{1,0:T(8,128)(2,1)S(1)} %shard_map.132.refs_0_, ...), custom_call_target="tpu_custom_call", output_to_operand_aliasing={{0}: (5, {}), {1}: (6, {})} | custom-call | flops 1258291200 | bytes 4751360 | tf_op jit(solution)/shard_map/pallas_call | solution.py:394
  167.0 5.4 %shard_map.139 = bf16[3,320,2048]{2,1,0:T(8,128)(2,1)} custom-call(s32[2]{0:T(128)S(1)} %pad_add_fusion.3.where_ref, f32[1,1280]{1,0:T(1,128)S(1)} %broadcast_in_dim.6.gain_ref, bf16[960,1280]{1,0:T(8,128)(2,1)} %bitcast.54, bf16[512,640]{1,0:T(8,128)(2,1)} %collective-permute-done.35.refs_0_, ...), custom_call_target="tpu_custom_call", output_to_operand_aliasing={{}: (5, {})} | custom-call | flops 1258291200 | bytes 4751360 | tf_op jit(solution)/shard_map/pallas_call | solution.py:394
  (115 shorter events, 40.5 us)
Async XLA Ops:
  0.7 21.6 %collective-permute-start.3 = (bf16[1280,1280]{1,0:T(8,128)(2,1)}, bf16[1280,1280]{1,0:T(8,128)(2,1)}, u32[]{:S(2)}, u32[]{:S(2)}) collective-permute-start(bf16[1280,1280]{1,0:T(8,128)(2,1)} %bitcast.40), channel_id=1, source_target_pairs={{0,8},{8,0},{16,24},{24,16},{1,9},{9,1},{17,25},{25,17},{2,10},{10... | collective-permute-start | bytes 9830408 | tf_op jit(solution)/shard_map/ppermute | solution.py:32
  1.2 21.1 %collective-permute-start.4 = (bf16[1280,1280]{1,0:T(8,128)(2,1)}, bf16[1280,1280]{1,0:T(8,128)(2,1)}, u32[]{:S(2)}, u32[]{:S(2)}) collective-permute-start(bf16[1280,1280]{1,0:T(8,128)(2,1)} %bitcast.45), channel_id=1, source_target_pairs={{0,8},{8,0},{16,24},{24,16},{1,9},{9,1},{17,25},{25,17},{2,10},{10... | collective-permute-start | bytes 9830408 | tf_op jit(solution)/shard_map/ppermute | solution.py:32
  2.0 17.8 %collective-permute-start = (bf16[512,640]{1,0:T(8,128)(2,1)S(1)}, bf16[512,640]{1,0:T(8,128)(2,1)}, u32[]{:S(2)}, u32[]{:S(2)}) collective-permute-start(bf16[512,640]{1,0:T(8,128)(2,1)S(1)} %constant_dynamic-slice_fusion.1), channel_id=1, source_target_pairs={{0,16},{8,24},{16,0},{24,8},{1,17},{9,25},{17,1},{25,9},{2,18},{10... | collective-permute-start | bytes 1966088 | tf_op jit(solution)/shard_map/ppermute | solution.py:32
  5.1 15.9 %collective-permute-start.1 = (bf16[512,640]{1,0:T(8,128)(2,1)S(1)}, bf16[512,640]{1,0:T(8,128)(2,1)}, u32[]{:S(2)}, u32[]{:S(2)}) collective-permute-start(bf16[512,640]{1,0:T(8,128)(2,1)S(1)} %constant_dynamic-slice_fusion.refs_0_), channel_id=1, source_target_pairs={{0,8},{8,0},{16,24},{24,16},{1,9},{9,1},{17,25},{25,17},{2,10},{10... | collective-permute-start | bytes 1966088 | tf_op jit(solution)/shard_map/ppermute | solution.py:32
  31.8 13.8 %collective-permute-start.13 = (bf16[128,640]{1,0:T(8,128)(2,1)S(1)}, bf16[128,640]{1,0:T(8,128)(2,1)S(1)}, u32[]{:S(2)}, u32[]{:S(2)}) collective-permute-start(bf16[128,640]{1,0:T(8,128)(2,1)S(1)} %get-tuple-element.91), channel_id=1, source_target_pairs={{0,2},{1,3},{2,0},{3,1},{4,6},{5,7},{6,4},{7,5},{8,10},{9,11},{10,... | collective-permute-start | bytes 491528 | tf_op jit(solution)/shard_map/ppermute | solution.py:32
  33.4 13.4 %collective-permute-start.14 = (bf16[128,640]{1,0:T(8,128)(2,1)S(1)}, bf16[128,640]{1,0:T(8,128)(2,1)S(1)}, u32[]{:S(2)}, u32[]{:S(2)}) collective-permute-start(bf16[128,640]{1,0:T(8,128)(2,1)S(1)} %get-tuple-element.92), channel_id=1, source_target_pairs={{0,3},{1,2},{2,1},{3,0},{4,7},{5,6},{6,5},{7,4},{8,11},{9,10},{10,... | collective-permute-start | bytes 491528 | tf_op jit(solution)/shard_map/ppermute | solution.py:32
  33.5 15.0 %collective-permute-start.10 = (bf16[128,640]{1,0:T(8,128)(2,1)S(1)}, bf16[128,640]{1,0:T(8,128)(2,1)S(1)}, u32[]{:S(2)}, u32[]{:S(2)}) collective-permute-start(bf16[128,640]{1,0:T(8,128)(2,1)S(1)} %get-tuple-element.89), channel_id=1, source_target_pairs={{0,4},{1,5},{2,6},{3,7},{4,0},{5,1},{6,2},{7,3},{8,12},{9,13},{10,... | collective-permute-start | bytes 491528 | tf_op jit(solution)/shard_map/ppermute | solution.py:32
  36.5 15.2 %collective-permute-start.11 = (bf16[128,640]{1,0:T(8,128)(2,1)S(1)}, bf16[128,640]{1,0:T(8,128)(2,1)S(1)}, u32[]{:S(2)}, u32[]{:S(2)}) collective-permute-start(bf16[128,640]{1,0:T(8,128)(2,1)S(1)} %get-tuple-element.90), channel_id=1, source_target_pairs={{0,5},{1,4},{2,7},{3,6},{4,1},{5,0},{6,3},{7,2},{8,13},{9,12},{10,... | collective-permute-start | bytes 491528 | tf_op jit(solution)/shard_map/ppermute | solution.py:32
  37.8 15.5 %collective-permute-start.6 = (bf16[256,640]{1,0:T(8,128)(2,1)S(1)}, bf16[256,640]{1,0:T(8,128)(2,1)S(1)}, u32[]{:S(2)}, u32[]{:S(2)}) collective-permute-start(bf16[256,640]{1,0:T(8,128)(2,1)S(1)} %constant_dynamic-update-slice_fusion.refs_0_), channel_id=1, source_target_pairs={{0,16},{8,24},{16,0},{24,8},{1,17},{9,25},{17,1},{25,9},{2,18},{10... | collective-permute-start | bytes 983048 | tf_op jit(solution)/shard_map/ppermute | solution.py:32
  46.8 12.4 %collective-permute-start.15 = (bf16[256,640]{1,0:T(8,128)(2,1)S(1)}, bf16[256,640]{1,0:T(8,128)(2,1)S(1)}, u32[]{:S(2)}, u32[]{:S(2)}) collective-permute-start(bf16[256,640]{1,0:T(8,128)(2,1)S(1)} %constant_dynamic-update-slice_fusion.6.refs_0_), channel_id=1, source_target_pairs={{0,16},{8,24},{16,0},{24,8},{1,17},{9,25},{17,1},{25,9},{2,18},{10... | collective-permute-start | bytes 983048 | tf_op jit(solution)/shard_map/ppermute | solution.py:32
  51.7 17.9 %collective-permute-start.12 = (bf16[256,640]{1,0:T(8,128)(2,1)S(1)}, bf16[256,640]{1,0:T(8,128)(2,1)S(1)}, u32[]{:S(2)}, u32[]{:S(2)}) collective-permute-start(bf16[256,640]{1,0:T(8,128)(2,1)S(1)} %constant_dynamic-update-slice_fusion.4.refs_0_), channel_id=1, source_target_pairs={{0,16},{8,24},{16,0},{24,8},{1,17},{9,25},{17,1},{25,9},{2,18},{10... | collective-permute-start | bytes 983048 | tf_op jit(solution)/shard_map/ppermute | solution.py:32
  59.3 10.4 %collective-permute-start.7 = (bf16[128,640]{1,0:T(8,128)(2,1)S(1)}, bf16[128,640]{1,0:T(8,128)(2,1)S(1)}, u32[]{:S(2)}, u32[]{:S(2)}) collective-permute-start(bf16[128,640]{1,0:T(8,128)(2,1)S(1)} %get-tuple-element.87), channel_id=1, source_target_pairs={{0,6},{1,7},{2,4},{3,5},{4,2},{5,3},{6,0},{7,1},{8,14},{9,15},{10,... | collective-permute-start | bytes 491528 | tf_op jit(solution)/shard_map/ppermute | solution.py:32
  77.9 9.3 %collective-permute-start.19 = (bf16[256,640]{1,0:T(8,128)(2,1)S(1)}, bf16[256,640]{1,0:T(8,128)(2,1)S(1)}, u32[]{:S(2)}, u32[]{:S(2)}) collective-permute-start(bf16[256,640]{1,0:T(8,128)(2,1)S(1)} %get-tuple-element.100), channel_id=1, source_target_pairs={{0,16},{8,24},{16,0},{24,8},{1,17},{9,25},{17,1},{25,9},{2,18},{10... | collective-permute-start | bytes 983048 | tf_op jit(solution)/shard_map/ppermute | solution.py:32
  85.4 10.7 %collective-permute-start.16 = (bf16[256,640]{1,0:T(8,128)(2,1)S(1)}, bf16[256,640]{1,0:T(8,128)(2,1)S(1)}, u32[]{:S(2)}, u32[]{:S(2)}) collective-permute-start(bf16[256,640]{1,0:T(8,128)(2,1)S(1)} %get-tuple-element.104), channel_id=1, source_target_pairs={{0,16},{8,24},{16,0},{24,8},{1,17},{9,25},{17,1},{25,9},{2,18},{10... | collective-permute-start | bytes 983048 | tf_op jit(solution)/shard_map/ppermute | solution.py:32
  87.3 15.9 %collective-permute-start.20 = (bf16[256,640]{1,0:T(8,128)(2,1)S(1)}, bf16[256,640]{1,0:T(8,128)(2,1)S(1)}, u32[]{:S(2)}, u32[]{:S(2)}) collective-permute-start(bf16[256,640]{1,0:T(8,128)(2,1)S(1)} %get-tuple-element.114), channel_id=1, source_target_pairs={{0,16},{8,24},{16,0},{24,8},{1,17},{9,25},{17,1},{25,9},{2,18},{10... | collective-permute-start | bytes 983048 | tf_op jit(solution)/shard_map/ppermute | solution.py:32
  96.2 11.2 %collective-permute-start.17 = (bf16[256,640]{1,0:T(8,128)(2,1)S(1)}, bf16[256,640]{1,0:T(8,128)(2,1)S(1)}, u32[]{:S(2)}, u32[]{:S(2)}) collective-permute-start(bf16[256,640]{1,0:T(8,128)(2,1)S(1)} %get-tuple-element.108), channel_id=1, source_target_pairs={{0,16},{8,24},{16,0},{24,8},{1,17},{9,25},{17,1},{25,9},{2,18},{10... | collective-permute-start | bytes 983048 | tf_op jit(solution)/shard_map/ppermute | solution.py:32
  98.0 11.3 %collective-permute-start.23 = (bf16[128,640]{1,0:T(8,128)(2,1)S(1)}, bf16[128,640]{1,0:T(8,128)(2,1)S(1)}, u32[]{:S(2)}, u32[]{:S(2)}) collective-permute-start(bf16[128,640]{1,0:T(8,128)(2,1)S(1)} %get-tuple-element.111), channel_id=1, source_target_pairs={{0,4},{1,5},{2,6},{3,7},{4,0},{5,1},{6,2},{7,3},{8,12},{9,13},{10,... | collective-permute-start | bytes 491528 | tf_op jit(solution)/shard_map/ppermute | solution.py:32
  100.5 14.3 %collective-permute-start.24 = (bf16[128,640]{1,0:T(8,128)(2,1)S(1)}, bf16[128,640]{1,0:T(8,128)(2,1)S(1)}, u32[]{:S(2)}, u32[]{:S(2)}) collective-permute-start(bf16[128,640]{1,0:T(8,128)(2,1)S(1)} %get-tuple-element.112), channel_id=1, source_target_pairs={{0,5},{1,4},{2,7},{3,6},{4,1},{5,0},{6,3},{7,2},{8,13},{9,12},{10,... | collective-permute-start | bytes 491528 | tf_op jit(solution)/shard_map/ppermute | solution.py:32
  103.3 13.4 %collective-permute-start.21 = (bf16[128,640]{1,0:T(8,128)(2,1)S(1)}, bf16[128,640]{1,0:T(8,128)(2,1)S(1)}, u32[]{:S(2)}, u32[]{:S(2)}) collective-permute-start(bf16[128,640]{1,0:T(8,128)(2,1)S(1)} %get-tuple-element.115), channel_id=1, source_target_pairs={{0,2},{1,3},{2,0},{3,1},{4,6},{5,7},{6,4},{7,5},{8,10},{9,11},{10,... | collective-permute-start | bytes 491528 | tf_op jit(solution)/shard_map/ppermute | solution.py:32
  107.4 10.0 %collective-permute-start.25 = (bf16[128,640]{1,0:T(8,128)(2,1)S(1)}, bf16[128,640]{1,0:T(8,128)(2,1)S(1)}, u32[]{:S(2)}, u32[]{:S(2)}) collective-permute-start(bf16[128,640]{1,0:T(8,128)(2,1)S(1)} %get-tuple-element.105), channel_id=1, source_target_pairs={{0,6},{1,7},{2,4},{3,5},{4,2},{5,3},{6,0},{7,1},{8,14},{9,15},{10,... | collective-permute-start | bytes 491528 | tf_op jit(solution)/shard_map/ppermute | solution.py:32
  109.2 11.0 %collective-permute-start.26 = (bf16[128,640]{1,0:T(8,128)(2,1)S(1)}, bf16[128,640]{1,0:T(8,128)(2,1)S(1)}, u32[]{:S(2)}, u32[]{:S(2)}) collective-permute-start(bf16[128,640]{1,0:T(8,128)(2,1)S(1)} %get-tuple-element.106), channel_id=1, source_target_pairs={{0,7},{1,6},{2,5},{3,4},{4,3},{5,2},{6,1},{7,0},{8,15},{9,14},{10,... | collective-permute-start | bytes 491528 | tf_op jit(solution)/shard_map/ppermute | solution.py:32
  127.4 17.1 %collective-permute-start.31 = (bf16[512,640]{1,0:T(8,128)(2,1)}, bf16[512,640]{1,0:T(8,128)(2,1)}, u32[]{:S(2)}, u32[]{:S(2)}) collective-permute-start(bf16[512,640]{1,0:T(8,128)(2,1)} %shard_map.135.refs_0_), channel_id=1, source_target_pairs={{0,16},{8,24},{16,0},{24,8},{1,17},{9,25},{17,1},{25,9},{2,18},{10... | collective-permute-start | bytes 1966088 | tf_op jit(solution)/shard_map/ppermute | solution.py:32
  144.5 9.3 %collective-permute-start.34 = (bf16[512,640]{1,0:T(8,128)(2,1)}, bf16[512,640]{1,0:T(8,128)(2,1)}, u32[]{:S(2)}, u32[]{:S(2)}) collective-permute-start(bf16[512,640]{1,0:T(8,128)(2,1)} %collective-permute-done.31.refs_1_), channel_id=1, source_target_pairs={{0,8},{8,0},{16,24},{24,16},{1,9},{9,1},{17,25},{25,17},{2,10},{10... | collective-permute-start | bytes 1966088 | tf_op jit(solution)/shard_map/ppermute | solution.py:32
  145.0 16.6 %collective-permute-start.32 = (bf16[512,640]{1,0:T(8,128)(2,1)S(1)}, bf16[512,640]{1,0:T(8,128)(2,1)S(1)}, u32[]{:S(2)}, u32[]{:S(2)}) collective-permute-start(bf16[512,640]{1,0:T(8,128)(2,1)S(1)} %shard_map.132.refs_0_), channel_id=1, source_target_pairs={{0,16},{8,24},{16,0},{24,8},{1,17},{9,25},{17,1},{25,9},{2,18},{10... | collective-permute-start | bytes 1966088 | tf_op jit(solution)/shard_map/ppermute | solution.py:32
  (23 other events, 262.6 us)
